TPU v7x, 32 devices: a whole 2x2x4 slice. The times are simulated.
32 devices in a mesh: expert: 4 (over x, core), tensor: 8 (over z, y).
Axes of the slice: x: 2, y: 2, z: 4, core: 2. Of those that a mesh axis runs over, the one named last changes fastest.
Arguments:
- resid: bfloat16 [2048, 2048], P(('expert', 'tensor')), may hold values from -6 to 6
- contexts: bfloat16 [2048, 4096], P('expert', 'tensor'), may hold values from -6 to 6
- att_routes: int32 [2048, 2], P('expert'), may hold values from 0 to 7, all different within a row
- att_scores: float32 [2048, 2], P('expert'), may hold values from -6 to 6
- att_out_w: bfloat16 [8, 2048, 2048], P(None, 'tensor'), may hold values from -0.125 to 0.125
- norm_gain: bfloat16 [2048], replicated, may hold values from 0.25 to 1.75
- router_w: bfloat16 [2048, 8], replicated, may hold values from -0.125 to 0.125
- mlp_routes: int32 [2048, 2], P(('expert', 'tensor')), may hold values from 0 to 7, all different within a row
- split_rule: int32 [2048, 2], P(('expert', 'tensor')), may hold values from 0 to 2519
- placement: int32 [8], replicated, may hold values from 0 to 7, as said below
- cap_blocks: int32 [8], replicated, may hold values from 1 to 2, as said below
- w_gate_up: bfloat16 [8, 2048, 2, 5632], P('tensor', None, None, 'expert'), as said below
- w_down: bfloat16 [8, 5632, 2048], P('tensor', 'expert'), as said below
- final_gain: bfloat16 [2048], replicated, may hold values from 0.25 to 1.75
Outputs:
- stream_out: bfloat16 [2048, 2048], P(('expert', 'tensor'))
- normalized: bfloat16 [2048, 2048], P(('expert', 'tensor'))
Inputs may be any that keep to these rules, and one draw needn't show every extreme that they name: `att_routes`: each row names 2 different experts. `mlp_routes`: each row names 2 different experts. `placement`: every expert is held by at least one slot. `cap_blocks`: some slot accepts 2 blocks. `w_gate_up`: slots that hold the same expert hold equal weights. `w_down`: slots that hold the same expert hold equal weights.
All inputs are finite; a program needn't handle non-finite values.
Results may differ from a plain program's by a relative error of at most 0.023.
Values may be sent and summed in bfloat16 or wider, within the bound.
A program may use at most 64 MiB of HBM per device.

v0:
```python
import jax
import jax.numpy as jnp
from jax import lax
from jax.sharding import PartitionSpec as P

MAXB = 2


norm_eps = 1e-06


def rms_norm(values, gain):
    scale = lax.rsqrt(jnp.mean(values * values, axis=-1, keepdims=True) + norm_eps)
    return values * scale * gain.astype(values.dtype)


def pair_gates(scores):
    first = jax.nn.silu(scores[:, 0:1] * 0.0) * 0.0 + jax.nn.sigmoid(
        scores[:, 0:1] - scores[:, 1:2]
    )
    first = first[:, 0]
    return jnp.stack([first, 1.0 - first], axis=1)


def activate(shard_piece, w_gate_up):
    both = jnp.einsum(
        "tsecd,sdgf->tsecgf", shard_piece, w_gate_up, preferred_element_type=jnp.float32
    )
    hidden = (jax.nn.silu(both[:, :, :, :, 0, :]) * both[:, :, :, :, 1, :]).astype(jnp.bfloat16)
    hidden = jnp.transpose(hidden, (0, 2, 3, 1, 4))
    return hidden.reshape(
        hidden.shape[0] * hidden.shape[1] * hidden.shape[2], hidden.shape[3], hidden.shape[4]
    )


def per_device(
    resid,
    contexts,
    att_routes,
    att_scores,
    att_out_w,
    norm_gain,
    router_w,
    mlp_routes,
    split_rule,
    placement,
    cap_blocks,
    w_gate_up,
    w_down,
    final_gain,
):
    n_tensor = lax.axis_size("tensor")
    row_count = resid.shape[0]
    model_width = resid.shape[1]
    group_rows = contexts.shape[0]
    att_experts = att_out_w.shape[0]
    slice_ctx = att_out_w.shape[1]
    top_count = att_routes.shape[1]
    gate_att = pair_gates(att_scores)
    chosen = (
        att_routes[:, :, None] == jnp.arange(att_experts, dtype=jnp.int32)[None, None, :]
    ).astype(jnp.float32)
    weighted = chosen * gate_att[:, :, None]
    context_part = contexts.reshape(group_rows, slice_ctx, top_count).astype(jnp.float32)
    mixed = (
        jnp.einsum("tke,tck->tec", weighted, context_part)
        .astype(jnp.bfloat16)
        .reshape(group_rows, att_experts * slice_ctx)
    )
    weight_flat = att_out_w.reshape(att_experts * slice_ctx, model_width)
    row_block = mixed
    attention = lax.psum_scatter(
        jnp.dot(row_block, weight_flat, preferred_element_type=jnp.float32).astype(jnp.bfloat16),
        "tensor",
        scatter_dimension=0,
        tiled=True,
    ).astype(jnp.float32)
    stream = (resid.astype(jnp.float32) + attention).astype(jnp.bfloat16)
    normed = rms_norm(stream.astype(jnp.float32), norm_gain).astype(jnp.bfloat16)
    logits = jnp.dot(normed, router_w, preferred_element_type=jnp.float32)
    gate_mlp = pair_gates(jnp.take_along_axis(logits, mlp_routes, axis=1))
    replicas = placement.shape[0]
    slots = w_gate_up.shape[0]
    expert_total = router_w.shape[1]
    block_rows = max(1, row_count * top_count // (2 * replicas))
    capacity_rows = MAXB * block_rows
    slot_ids = jnp.arange(replicas, dtype=jnp.int32)
    expert_ids = jnp.arange(expert_total, dtype=jnp.int32)
    copies = jnp.sum((placement[None, :] == expert_ids[:, None]).astype(jnp.int32), axis=1)
    earlier = jnp.sum(
        (
            (placement[None, :] == placement[:, None]) & (slot_ids[None, :] < slot_ids[:, None])
        ).astype(jnp.int32),
        axis=1,
    )
    route_onehot = (mlp_routes[:, :, None] == expert_ids[None, None, :]).astype(jnp.int32)
    route_copies = jnp.sum(route_onehot * copies[None, None, :], axis=2)
    replica_rank = jnp.remainder(split_rule, route_copies)
    match = (
        (placement[None, None, :] == mlp_routes[:, :, None])
        & (earlier[None, None, :] == replica_rank[:, :, None])
    ).astype(jnp.int32)
    replica_slot = jnp.sum(match * slot_ids[None, None, :], axis=2)
    capacity = jnp.sum(match * cap_blocks[None, None, :], axis=2) * block_rows
    flat_match = match.reshape(row_count * top_count, replicas)
    before = jnp.cumsum(flat_match, axis=0) - flat_match
    arrival = jnp.sum(before * flat_match, axis=1).reshape(row_count, top_count)
    is_kept = arrival < capacity
    holder = replica_slot // slots
    within = replica_slot % slots
    position = within * (n_tensor * capacity_rows) + holder * capacity_rows + arrival
    position = jnp.where(is_kept, position, -1)
    buffer_rows = slots * n_tensor * capacity_rows
    placer = jnp.sum(
        (jnp.arange(buffer_rows, dtype=jnp.int32)[:, None, None] == position[None, :, :]).astype(
            jnp.bfloat16
        ),
        axis=2,
    )
    send_rows = jnp.dot(placer, normed, preferred_element_type=jnp.float32).astype(jnp.bfloat16)
    send_rows = send_rows.reshape(slots, n_tensor, capacity_rows, model_width)
    collected = lax.all_gather(send_rows[None], "expert", axis=0, tiled=True)
    arrived = lax.all_to_all(collected, "tensor", split_axis=2, concat_axis=2, tiled=True)
    hidden = activate(arrived, w_gate_up)
    row_block = hidden
    summed = lax.psum_scatter(
        jnp.einsum("bsf,sfd->bsd", row_block, w_down, preferred_element_type=jnp.float32).astype(
            jnp.bfloat16
        ),
        "expert",
        scatter_dimension=0,
        tiled=True,
    )
    results = summed.reshape(n_tensor, capacity_rows, slots, model_width)
    returned = lax.all_to_all(results, "tensor", split_axis=0, concat_axis=0, tiled=True)
    flat_back = returned.reshape(n_tensor * capacity_rows * slots, model_width)
    back_index = jnp.where(is_kept, holder * (capacity_rows * slots) + arrival * slots + within, 0)
    fetched = (
        jnp.take(flat_back, back_index.reshape(-1), axis=0)
        .reshape(row_count, top_count, model_width)
        .astype(jnp.float32)
    )
    factors = gate_mlp * is_kept.astype(jnp.float32)
    expert_mix = fetched[:, 0, :] * factors[:, 0:1] + fetched[:, 1, :] * factors[:, 1:2]
    after = stream.astype(jnp.float32) + expert_mix
    return (after.astype(jnp.bfloat16), rms_norm(after, final_gain).astype(jnp.bfloat16))


def solution(mesh):
    return jax.shard_map(
        per_device,
        mesh=mesh,
        in_specs=(
            P(("expert", "tensor"), None),
            P("expert", "tensor"),
            P("expert", None),
            P("expert", None),
            P(None, "tensor", None),
            P(),
            P(),
            P(("expert", "tensor"), None),
            P(("expert", "tensor"), None),
            P(),
            P(),
            P("tensor", None, None, "expert"),
            P("tensor", "expert", None),
            P(),
        ),
        out_specs=(P(("expert", "tensor"), None), P(("expert", "tensor"), None)),
        check_vma=False,
    )
```

profile of v0, /device:TPU:0, one launch (start us, length us, event | category | flops | bytes accessed | tf_op | source)
XLA Modules:
  0.0 246.5 jit_solution(10322497343723658886)
XLA Ops:
  7.2 1.3 copy.74
  8.5 0.2 reshape.175
  8.7 1.0 copy.75
  10.1 3.9 %convolution_convert_fusion.1 = bf16[512,8,256]{2,1,0:T(8,128)(2,1)S(1)} fusion(bf16[512,256,2]{1,2,0:T(2,128)(2,1)S(1)} %copy.75, bf16[512,2]{1,0:T(8,128)(2,1)S(1)} %copy.73, s32[512,2]{1,0:T(8,128)S(1)} %copy.72), kind=kOutput, calls=%fused_computation.16 | convolution fusion | flops 4210688 | bytes 2627584 | tf_op jit(solution)/shard_map/tke,tck->tec/dot_general | solution.py:66
  14.1 5.7 %bitcast_convert_fusion = bf16[512,2048]{1,0:T(8,128)(2,1)} fusion(bf16[8,256,2048]{2,1,0:T(8,128)(2,1)S(1)} %copy-done.10, bf16[512,8,256]{2,1,0:T(8,128)(2,1)S(1)} %convolution_convert_fusion.1), kind=kOutput, calls=%fused_computation.7 | convolution fusion | flops 4296015872 | bytes 12582912 | tf_op jit(solution)/shard_map/dot_general | solution.py:73
  21.7 69.4 %reduce-scatter.3.cloned.1.call-done = bf16[64,2048]{1,0:T(8,128)(2,1)} async-done(((bf16[512,2048]{1,0:T(8,128)(2,1)}), bf16[64,2048]{1,0:T(8,128)(2,1)}) %reduce-scatter.3.cloned.1.call-update) | async-done | bytes 262160 | tf_op jit(solution)/shard_map/reduce_scatter | solution.py:72
  91.1 1.2 fusion.17
  92.3 1.2 convolution_convert_fusion
  93.5 21.7 %all-gather.2.cloned.1.call-done = bf16[4,1,8,16,2048]{4,3,2,1,0:T(8,128)(2,1)} async-done(((bf16[1,1,8,16,2048]{4,3,2,1,0:T(8,128)(2,1)}), bf16[4,1,8,16,2048]{4,3,2,1,0:T(8,128)(2,1)}) %all-gather.2.cloned.1.call-update) | async-done | bytes 2097168 | tf_op jit(solution)/shard_map/all_gather | solution.py:122
  115.2 1.8 copy.81
  117.0 54.2 %all_to_all.10 = bf16[4,1,8,16,2048]{4,3,0,1,2:T(8,128)(2,1)S(1)} all-to-all(bf16[4,1,8,16,2048]{4,3,0,1,2:T(8,128)(2,1)S(1)} %copy.81), channel_id=1, replica_groups=mesh['expert'=4,'tensor'=8] {'tensor'}, dimensions={2} | all-to-all | bytes 4194304 | tf_op jit(solution)/shard_map/all_to_all | solution.py:123
  171.2 10.6 %fusion.4 = f32[4,1,8,16,2,1408]{5,3,4,2,0,1:T(8,128)S(1)} fusion(bf16[2048,2,1408,1,1]{2,1,0,4,3:T(2,128)(2,1)} %bitcast.80, bf16[4,1,8,16,2048]{4,3,0,1,2:T(8,128)(2,1)S(1)} %all_to_all.10), kind=kOutput, calls=%fused_computation.6 | convolution fusion | flops 5905580032 | bytes 19398656 | tf_op jit(solution)/shard_map/tsecd,sdgf->tsecgf/dot_general | solution.py:26
  181.8 0.8 fusion.10
  182.7 4.7 %fusion.11 = bf16[512,1,2048]{2,0,1:T(8,128)(2,1)} fusion(bf16[512,1408]{1,0:T(8,128)(2,1)S(1)} %bitcast.78, bf16[1,1408,2048]{2,1,0:T(8,128)(2,1)S(1)} %bitcast.82), kind=kOutput, calls=%fused_computation.11 | convolution fusion | flops 2953838592 | bytes 9306112 | tf_op jit(solution)/shard_map/bsf,sfd->bsd/dot_general | solution.py:127
  188.2 29.0 %reduce-scatter.5.cloned.1.call-done = bf16[128,1,2048]{2,0,1:T(8,128)(2,1)} async-done(((bf16[512,1,2048]{2,0,1:T(8,128)(2,1)}), bf16[128,1,2048]{2,0,1:T(8,128)(2,1)}) %reduce-scatter.5.cloned.1.call-update) | async-done | bytes 524304 | tf_op jit(solution)/shard_map/reduce_scatter | solution.py:126
  217.2 5.5 %all-to-all-start.1 = ((bf16[8,16,1,2048]{3,1,2,0:T(8,128)(2,1)}), bf16[8,16,1,2048]{3,1,2,0:T(8,128)(2,1)S(1)}, u32[]{:S(2)}, u32[]{:S(2)}) async-start(bf16[8,16,1,2048]{3,1,2,0:T(8,128)(2,1)} %bitcast.79), calls=%async_computation.3 | async-start | bytes 1048576 | tf_op jit(solution)/shard_map/all_to_all | solution.py:135
  222.7 0.2 fusion.28
  223.0 1.0 gather_fusion.1
  224.3 12.9 %all-to-all-done.1 = bf16[8,16,1,2048]{3,1,2,0:T(8,128)(2,1)S(1)} async-done(((bf16[8,16,1,2048]{3,1,2,0:T(8,128)(2,1)}), bf16[8,16,1,2048]{3,1,2,0:T(8,128)(2,1)S(1)}, u32[]{:S(2)}, u32[]{:S(2)}) %all-to-all-start.1) | async-done | bytes 524320 | tf_op jit(solution)/shard_map/all_to_all | solution.py:135
  237.2 0.9 gather_fusion
  238.2 0.3 gather.11
  238.5 0.3 fusion.23
  238.9 0.3 multiply_reduce_fusion
  239.2 0.8 multiply_convert_fusion
  (72 shorter events, 3.3 us)
Async XLA Ops:
  7.2 215.6 %copy-start = (bf16[2048,8]{0,1:T(8,128)(2,1)S(1)}, bf16[2048,8]{0,1:T(8,128)(2,1)}, u32[]{:S(2)}) copy-start(bf16[2048,8]{0,1:T(8,128)(2,1)} %param.20) | copy-start | bytes 98308
  7.2 2.5 %copy-start.7 = (f32[512,2]{0,1:T(2,128)S(1)}, f32[512,2]{0,1:T(2,128)}, u32[]{:S(2)}) copy-start(f32[512,2]{0,1:T(2,128)} %param.17) | copy-start | bytes 12292
  7.2 2.8 %copy-start.4 = (s32[512,2]{0,1:T(2,128)S(1)}, s32[512,2]{0,1:T(2,128)}, u32[]{:S(2)}) copy-start(s32[512,2]{0,1:T(2,128)} %param.16) | copy-start | bytes 12292
  7.2 83.9 %reduce-scatter.3.cloned.1.call-start = ((), (), s32[]{:S(2)}) async-start(), calls=%async_computation.4 | async-start | bytes 2359296 | tf_op jit(solution)/shard_map/reduce_scatter | solution.py:72
  10.1 3.9 %copy-start.10 = (bf16[8,256,2048]{2,1,0:T(8,128)(2,1)S(1)}, bf16[8,256,2048]{2,1,0:T(8,128)(2,1)}, u32[]{:S(2)}) copy-start(bf16[8,256,2048]{2,1,0:T(8,128)(2,1)} %param.18) | copy-start | bytes 25165828
  14.0 5.9 %copy-start.5 = (bf16[2048]{0:T(1024)(128)(2,1)S(1)}, bf16[2048]{0:T(1024)(128)(2,1)}, u32[]{:S(2)}) copy-start(bf16[2048]{0:T(1024)(128)(2,1)} %param.19) | copy-start | bytes 12292
  14.1 5.9 %copy-start.2 = (s32[64,2]{0,1:T(2,128)S(1)}, s32[64,2]{0,1:T(2,128)}, u32[]{:S(2)}) copy-start(s32[64,2]{0,1:T(2,128)} %param.21) | copy-start | bytes 1540
  14.1 6.0 %copy-start.3 = (s32[8]{0:T(128)S(1)}, s32[8]{0:T(128)}, u32[]{:S(2)}) copy-start(s32[8]{0:T(128)} %param.23) | copy-start | bytes 100
  14.1 6.2 %copy-start.8 = (s32[64,2]{0,1:T(2,128)S(1)}, s32[64,2]{0,1:T(2,128)}, u32[]{:S(2)}) copy-start(s32[64,2]{0,1:T(2,128)} %param.22) | copy-start | bytes 1540
  14.1 7.4 %copy-start.9 = (s32[8]{0:T(128)S(1)}, s32[8]{0:T(128)}, u32[]{:S(2)}) copy-start(s32[8]{0:T(128)} %param.24) | copy-start | bytes 100
  14.1 77.0 %copy-start.1 = (bf16[64,2048]{1,0:T(8,128)(2,1)S(1)}, bf16[64,2048]{1,0:T(8,128)(2,1)}, u32[]{:S(2)}) copy-start(bf16[64,2048]{1,0:T(8,128)(2,1)} %param.14) | copy-start | bytes 786436
  19.9 95.3 %all-gather.2.cloned.1.call-start = ((), (), s32[]{:S(2)}) async-start(), calls=%async_computation.5 | async-start | bytes 2621440 | tf_op jit(solution)/shard_map/all_gather | solution.py:122
  93.5 123.8 %reduce-scatter.5.cloned.1.call-start = ((), (), s32[]{:S(2)}) async-start(), calls=%async_computation.6 | async-start | bytes 2621440 | tf_op jit(solution)/shard_map/reduce_scatter | solution.py:126
  117.0 65.6 %slice-start = ((s8[5767168]{0:T(1024)(128)(4,1)}), s8[4194304]{0:T(1024)(128)(4,1)S(1)}, s32[]{:S(2)}) async-start(s8[5767168]{0:T(1024)(128)(4,1)} %bitcast.81), calls=%async_computation.7 | async-start | bytes 8388608
  171.2 11.5 %slice-start.1 = ((s8[5767168]{0:T(1024)(128)(4,1)}), s8[1572864]{0:T(1024)(128)(4,1)S(1)}, s32[]{:S(2)}) async-start(s8[5767168]{0:T(1024)(128)(4,1)} %bitcast.81), calls=%async_computation.8 | async-start | bytes 3145728
  182.7 5.5 %copy-start.6 = (bf16[2048]{0:T(1024)(128)(2,1)S(1)}, bf16[2048]{0:T(1024)(128)(2,1)}, u32[]{:S(2)}) copy-start(bf16[2048]{0:T(1024)(128)(2,1)} %param.27) | copy-start | bytes 12292
  217.2 20.0 %all-to-all-start.1 = ((bf16[8,16,1,2048]{3,1,2,0:T(8,128)(2,1)}), bf16[8,16,1,2048]{3,1,2,0:T(8,128)(2,1)S(1)}, u32[]{:S(2)}, u32[]{:S(2)}) async-start(bf16[8,16,1,2048]{3,1,2,0:T(8,128)(2,1)} %bitcast.79), calls=%async_computation.3 | async-start | bytes 1048576 | tf_op jit(solution)/shard_map/all_to_all | solution.py:135
Sparse Core Ops, SparseCore 0:
  20.0 71.0 reduce-scatter.2
  93.6 21.5 all-gather.1
  187.6 29.5 reduce-scatter.4
where the time goes:
time: 247 us
  waiting for transfers between devices  133 us (54%)
  blocking collectives  54.2 us (22%)
  matrix products  26.4 us (11%)
  between operations  14.2 us (6%)
  local copies, waits for them, and re-layouts  8.56 us (3%)
  starting transfers between devices  5.63 us (2%)
  other arithmetic  4.63 us (2%)
    reduce_scatter x1, waiting for transfers between devices, per_device(): lax.psum_scatter(jnp.dot(row_block, weight_flat, preferred_element_type=j...  69.4 us
    all_to_all x1, blocking collectives, per_device(): lax.all_to_all(collected, 'tensor', split_axis=2, concat_axis=2, tiled=True)  54.2 us
    reduce_scatter x1, waiting for transfers between devices, per_device(): lax.psum_scatter(jnp.einsum('bsf,sfd->bsd', row_block, w_down, preferred_...  29 us
    all_gather x1, waiting for transfers between devices, per_device(): collected = lax.all_gather(send_rows[None], 'expert', axis=0, tiled=True)  21.7 us
    all_to_all x1, waiting for transfers between devices, per_device(): lax.all_to_all(results, 'tensor', split_axis=0, concat_axis=0, tiled=True)  12.9 us
    dot_general x1, matrix products, activate(): jnp.einsum('tsecd,sdgf->tsecgf', shard_piece, w_gate_up, preferred_elemen...  10.6 us
    dot_general x1, matrix products, per_device(): jnp.dot(row_block, weight_flat, preferred_element_type=jnp.float32)  5.73 us
    all_to_all x1, starting transfers between devices, per_device(): lax.all_to_all(results, 'tensor', split_axis=0, concat_axis=0, tiled=True)  5.51 us
  transfers between devices with their start and end apart: 4, of which 4 were waited for; matrix products, arithmetic and copies ran while one was open for 2% of the time, Pallas kernels for 0%

commit v1 on v0

--- a/solution.py
+++ b/solution.py
@@ -119,8 +119,8 @@
     )
     send_rows = jnp.dot(placer, normed, preferred_element_type=jnp.float32).astype(jnp.bfloat16)
     send_rows = send_rows.reshape(slots, n_tensor, capacity_rows, model_width)
-    collected = lax.all_gather(send_rows[None], "expert", axis=0, tiled=True)
-    arrived = lax.all_to_all(collected, "tensor", split_axis=2, concat_axis=2, tiled=True)
+    landed = lax.all_to_all(send_rows, "tensor", split_axis=1, concat_axis=1, tiled=True)
+    arrived = lax.all_gather(landed[None], "expert", axis=0, tiled=True)
     hidden = activate(arrived, w_gate_up)
     row_block = hidden
     summed = lax.psum_scatter(

time: 247 us -> 212 us (0.86)
  blocking collectives: 54.2 us -> 16.8 us
  matrix products: 26.4 us -> 29.1 us
    all_to_all x1, blocking collectives: 54.2 us -> 16.8 us  [per_device(): lax.all_to_all(send_rows, 'tensor', split_axis=1, concat_axis=1, tiled=True)]
    dot_general x1, matrix products: 4.73 us -> 7.47 us  [per_device(): jnp.einsum('bsf,sfd->bsd', row_block, w_down, preferred_element_type=jnp....]
where the time goes in v1:
time: 212 us
  waiting for transfers between devices  135 us (64%)
  matrix products  29.1 us (14%)
  blocking collectives  16.8 us (8%)
  between operations  14.1 us (7%)
  local copies, waits for them, and re-layouts  6.73 us (3%)
  starting transfers between devices  5.64 us (3%)
  other arithmetic  4.68 us (2%)
    reduce_scatter x1, waiting for transfers between devices, per_device(): lax.psum_scatter(jnp.dot(row_block, weight_flat, preferred_element_type=j...  69.4 us
    reduce_scatter x1, waiting for transfers between devices, per_device(): lax.psum_scatter(jnp.einsum('bsf,sfd->bsd', row_block, w_down, preferred_...  30.9 us
    all_gather x1, waiting for transfers between devices, per_device(): arrived = lax.all_gather(landed[None], 'expert', axis=0, tiled=True)  21.7 us
    all_to_all x1, blocking collectives, per_device(): lax.all_to_all(send_rows, 'tensor', split_axis=1, concat_axis=1, tiled=True)  16.8 us
    all_to_all x1, waiting for transfers between devices, per_device(): lax.all_to_all(results, 'tensor', split_axis=0, concat_axis=0, tiled=True)  12.9 us
    dot_general x1, matrix products, activate(): jnp.einsum('tsecd,sdgf->tsecgf', shard_piece, w_gate_up, preferred_elemen...  11.4 us
    dot_general x1, matrix products, per_device(): jnp.einsum('bsf,sfd->bsd', row_block, w_down, preferred_element_type=jnp....  7.47 us
    dot_general x1, matrix products, per_device(): jnp.dot(row_block, weight_flat, preferred_element_type=jnp.float32)  5.73 us
  transfers between devices with their start and end apart: 4, of which 4 were waited for; matrix products, arithmetic and copies ran while one was open for 2% of the time, Pallas kernels for 0%

profile of v1, /device:TPU:0, one launch (start us, length us, event | category | flops | bytes accessed | tf_op | source)
XLA Modules:
  0.0 212.0 jit_solution(8811319731959321057)
XLA Ops:
  7.2 1.3 copy.72
  8.5 0.2 reshape.178
  8.7 1.0 copy.73
  9.8 0.2 copy.71
  10.1 3.9 %convolution_convert_fusion.1 = bf16[512,8,256]{2,1,0:T(8,128)(2,1)S(1)} fusion(bf16[512,256,2]{1,2,0:T(2,128)(2,1)S(1)} %copy.73, bf16[512,2]{1,0:T(8,128)(2,1)S(1)} %copy.71, s32[512,2]{1,0:T(8,128)S(1)} %copy.70), kind=kOutput, calls=%fused_computation.15 | convolution fusion | flops 4210688 | bytes 2627584 | tf_op jit(solution)/shard_map/tke,tck->tec/dot_general | solution.py:66
  14.1 5.7 %bitcast_convert_fusion = bf16[512,2048]{1,0:T(8,128)(2,1)} fusion(bf16[8,256,2048]{2,1,0:T(8,128)(2,1)S(1)} %copy-done.10, bf16[512,8,256]{2,1,0:T(8,128)(2,1)S(1)} %convolution_convert_fusion.1), kind=kOutput, calls=%fused_computation.7 | convolution fusion | flops 4296015872 | bytes 12582912 | tf_op jit(solution)/shard_map/dot_general | solution.py:73
  21.7 69.4 %reduce-scatter.3.cloned.1.call-done = bf16[64,2048]{1,0:T(8,128)(2,1)} async-done(((bf16[512,2048]{1,0:T(8,128)(2,1)}), bf16[64,2048]{1,0:T(8,128)(2,1)}) %reduce-scatter.3.cloned.1.call-update) | async-done | bytes 262160 | tf_op jit(solution)/shard_map/reduce_scatter | solution.py:72
  91.1 1.2 fusion.16
  92.3 0.4 convolution_convert_fusion
  92.6 16.8 %all_to_all.10 = bf16[1,8,16,2048]{3,2,0,1:T(8,128)(2,1)} all-to-all(bf16[1,8,16,2048]{3,2,0,1:T(8,128)(2,1)S(1)} %bitcast.80), channel_id=1, replica_groups=mesh['expert'=4,'tensor'=8] {'tensor'}, dimensions={1} | all-to-all | bytes 1048576 | tf_op jit(solution)/shard_map/all_to_all | solution.py:122
  109.5 21.7 %all-gather.3.cloned.1.call-done = bf16[4,8,16,2048]{3,2,1,0:T(8,128)(2,1)} async-done(((bf16[1,8,16,2048]{3,2,1,0:T(8,128)(2,1)}), bf16[4,8,16,2048]{3,2,1,0:T(8,128)(2,1)}) %all-gather.3.cloned.1.call-update) | async-done | bytes 2097168 | tf_op jit(solution)/shard_map/all_gather | solution.py:123
  131.2 11.4 %fusion.4 = f32[4,1,8,16,2,1408]{5,3,4,2,0,1:T(8,128)S(1)} fusion(bf16[2048,2,1408,1,1]{2,1,0,4,3:T(2,128)(2,1)} %bitcast.83, bf16[4,8,16,2048]{3,2,1,0:T(8,128)(2,1)} %all-gather.3.cloned.1.call-done), kind=kOutput, calls=%fused_computation.6 | convolution fusion | flops 5905580032 | bytes 19398656 | tf_op jit(solution)/shard_map/tsecd,sdgf->tsecgf/dot_general | solution.py:26
  142.7 0.9 fusion.10
  143.5 7.5 %fusion.11 = bf16[512,1,2048]{2,0,1:T(8,128)(2,1)} fusion(bf16[512,1408]{1,0:T(8,128)(2,1)S(1)} %bitcast.81, bf16[1,1408,2048]{2,1,0:T(8,128)(2,1)} %param.26), kind=kOutput, calls=%fused_computation.11 | convolution fusion | flops 2953838592 | bytes 9306112 | tf_op jit(solution)/shard_map/bsf,sfd->bsd/dot_general | solution.py:127
  151.8 30.9 %reduce-scatter.5.cloned.1.call-done = bf16[128,1,2048]{2,0,1:T(8,128)(2,1)} async-done(((bf16[512,1,2048]{2,0,1:T(8,128)(2,1)}), bf16[128,1,2048]{2,0,1:T(8,128)(2,1)}) %reduce-scatter.5.cloned.1.call-update) | async-done | bytes 524304 | tf_op jit(solution)/shard_map/reduce_scatter | solution.py:126
  182.7 5.5 %all-to-all-start.1 = ((bf16[8,16,1,2048]{3,1,2,0:T(8,128)(2,1)}), bf16[8,16,1,2048]{3,1,2,0:T(8,128)(2,1)S(1)}, u32[]{:S(2)}, u32[]{:S(2)}) async-start(bf16[8,16,1,2048]{3,1,2,0:T(8,128)(2,1)} %bitcast.82), calls=%async_computation.3 | async-start | bytes 1048576 | tf_op jit(solution)/shard_map/all_to_all | solution.py:135
  188.2 0.2 fusion.27
  188.5 1.0 gather_fusion.1
  189.8 12.9 %all-to-all-done.1 = bf16[8,16,1,2048]{3,1,2,0:T(8,128)(2,1)S(1)} async-done(((bf16[8,16,1,2048]{3,1,2,0:T(8,128)(2,1)}), bf16[8,16,1,2048]{3,1,2,0:T(8,128)(2,1)S(1)}, u32[]{:S(2)}, u32[]{:S(2)}) %all-to-all-start.1) | async-done | bytes 524320 | tf_op jit(solution)/shard_map/all_to_all | solution.py:135
  202.7 0.9 gather_fusion
  203.6 0.3 gather.11
  204.0 0.3 fusion.22
  204.3 0.3 multiply_reduce_fusion
  204.6 0.8 multiply_convert_fusion
  (66 shorter events, 3.1 us)
Async XLA Ops:
  7.2 181.0 %copy-start = (bf16[2048,8]{0,1:T(8,128)(2,1)S(1)}, bf16[2048,8]{0,1:T(8,128)(2,1)}, u32[]{:S(2)}) copy-start(bf16[2048,8]{0,1:T(8,128)(2,1)} %param.20) | copy-start | bytes 98308
  7.2 2.5 %copy-start.7 = (f32[512,2]{0,1:T(2,128)S(1)}, f32[512,2]{0,1:T(2,128)}, u32[]{:S(2)}) copy-start(f32[512,2]{0,1:T(2,128)} %param.17) | copy-start | bytes 12292
  7.2 2.8 %copy-start.4 = (s32[512,2]{0,1:T(2,128)S(1)}, s32[512,2]{0,1:T(2,128)}, u32[]{:S(2)}) copy-start(s32[512,2]{0,1:T(2,128)} %param.16) | copy-start | bytes 12292
  7.2 83.9 %reduce-scatter.3.cloned.1.call-start = ((), (), s32[]{:S(2)}) async-start(), calls=%async_computation.4 | async-start | bytes 2359296 | tf_op jit(solution)/shard_map/reduce_scatter | solution.py:72
  10.1 3.9 %copy-start.10 = (bf16[8,256,2048]{2,1,0:T(8,128)(2,1)S(1)}, bf16[8,256,2048]{2,1,0:T(8,128)(2,1)}, u32[]{:S(2)}) copy-start(bf16[8,256,2048]{2,1,0:T(8,128)(2,1)} %param.18) | copy-start | bytes 25165828
  14.0 5.9 %copy-start.5 = (bf16[2048]{0:T(1024)(128)(2,1)S(1)}, bf16[2048]{0:T(1024)(128)(2,1)}, u32[]{:S(2)}) copy-start(bf16[2048]{0:T(1024)(128)(2,1)} %param.19) | copy-start | bytes 12292
  14.1 5.9 %copy-start.2 = (s32[64,2]{0,1:T(2,128)S(1)}, s32[64,2]{0,1:T(2,128)}, u32[]{:S(2)}) copy-start(s32[64,2]{0,1:T(2,128)} %param.21) | copy-start | bytes 1540
  14.1 6.0 %copy-start.3 = (s32[8]{0:T(128)S(1)}, s32[8]{0:T(128)}, u32[]{:S(2)}) copy-start(s32[8]{0:T(128)} %param.23) | copy-start | bytes 100
  14.1 6.2 %copy-start.8 = (s32[64,2]{0,1:T(2,128)S(1)}, s32[64,2]{0,1:T(2,128)}, u32[]{:S(2)}) copy-start(s32[64,2]{0,1:T(2,128)} %param.22) | copy-start | bytes 1540
  14.1 7.4 %copy-start.9 = (s32[8]{0:T(128)S(1)}, s32[8]{0:T(128)}, u32[]{:S(2)}) copy-start(s32[8]{0:T(128)} %param.24) | copy-start | bytes 100
  14.1 77.0 %copy-start.1 = (bf16[64,2048]{1,0:T(8,128)(2,1)S(1)}, bf16[64,2048]{1,0:T(8,128)(2,1)}, u32[]{:S(2)}) copy-start(bf16[64,2048]{1,0:T(8,128)(2,1)} %param.14) | copy-start | bytes 786436
  19.9 111.4 %all-gather.3.cloned.1.call-start = ((), (), s32[]{:S(2)}) async-start(), calls=%async_computation.6 | async-start | bytes 2621440 | tf_op jit(solution)/shard_map/all_gather | solution.py:123
  109.5 73.2 %reduce-scatter.5.cloned.1.call-start = ((), (), s32[]{:S(2)}) async-start(), calls=%async_computation.5 | async-start | bytes 2621440 | tf_op jit(solution)/shard_map/reduce_scatter | solution.py:126
  143.5 8.2 %copy-start.6 = (bf16[2048]{0:T(1024)(128)(2,1)S(1)}, bf16[2048]{0:T(1024)(128)(2,1)}, u32[]{:S(2)}) copy-start(bf16[2048]{0:T(1024)(128)(2,1)} %param.27) | copy-start | bytes 12292
  182.7 20.0 %all-to-all-start.1 = ((bf16[8,16,1,2048]{3,1,2,0:T(8,128)(2,1)}), bf16[8,16,1,2048]{3,1,2,0:T(8,128)(2,1)S(1)}, u32[]{:S(2)}, u32[]{:S(2)}) async-start(bf16[8,16,1,2048]{3,1,2,0:T(8,128)(2,1)} %bitcast.82), calls=%async_computation.3 | async-start | bytes 1048576 | tf_op jit(solution)/shard_map/all_to_all | solution.py:135
Sparse Core Ops, SparseCore 0:
  20.0 71.0 reduce-scatter.2
  109.6 21.5 all-gather.2
  151.2 31.4 reduce-scatter.4

commit v2 on v1

--- a/solution.py
+++ b/solution.py
@@ -1,7 +1,13 @@
+import functools
+
 import jax
 import jax.numpy as jnp
 from jax import lax
+from jax.experimental import pallas as pl
+from jax.experimental.pallas import tpu as pltpu
 from jax.sharding import PartitionSpec as P
+
+MESH = pl.DeviceIdType.MESH
 
 MAXB = 2
 
@@ -146,9 +152,409 @@
     return (after.astype(jnp.bfloat16), rms_norm(after, final_gain).astype(jnp.bfloat16))
 
 
+def greet(n_e, n_t):
+    e, t = lax.axis_index("expert"), lax.axis_index("tensor")
+    barrier = pltpu.get_barrier_semaphore()
+    for d in range(1, n_t):
+        pl.semaphore_signal(
+            barrier, inc=1, device_id=(e, lax.rem(t + d, n_t)), device_id_type=MESH
+        )
+    for d in range(1, n_e):
+        pl.semaphore_signal(
+            barrier, inc=1, device_id=(lax.rem(e + d, n_e), t), device_id_type=MESH
+        )
+    pl.semaphore_wait(barrier, n_t + n_e - 2)
+
+
+def send(src, dst, send_sem, recv_sem, device):
+    return pltpu.make_async_remote_copy(
+        src_ref=src,
+        dst_ref=dst,
+        send_sem=send_sem,
+        recv_sem=recv_sem,
+        device_id=device,
+        device_id_type=MESH,
+    )
+
+
+def front_kernel(
+    n_e, n_t, n_c, cap,
+    ctx_ref, routes_ref, scores_ref, w_hbm, resid_ref, gain_ref, router_ref, pick_ref, placer_ref,
+    rows_hbm, stream_ref, gate_ref,
+    w, mixed, q_send, q_recv, s_send, s_recv, own, d_send, held,
+    w_sem, out_sem, qs, qr, ss, sr, ds, dr, xs, xr, cs, cr, fs, fr,
+):
+    e, t = lax.axis_index("expert"), lax.axis_index("tensor")
+    n_z = n_t // 2
+    z, y = t // 2, lax.rem(t, 2)
+    other = t + 1 - 2 * y
+    cross, sibling = lax.rem(e + 2, 4), e + 1 - 2 * lax.rem(e, 2)
+    rows = resid_ref.shape[0]
+    cols = w.shape[2]
+    slice_ctx = ctx_ref.shape[3] // 2
+    experts = w.shape[1] // slice_ctx
+
+    def w_copy(c):
+        return pltpu.make_async_copy(
+            w_hbm.at[:, pl.ds(c * cols, cols)], w.at[c], w_sem.at[c]
+        )
+
+    for c in range(n_c):
+        w_copy(c).start()
+    greet(n_e, n_t)
+
+    j = lax.broadcasted_iota(jnp.int32, (2 * slice_ctx, slice_ctx), 0)
+    f = lax.broadcasted_iota(jnp.int32, (2 * slice_ctx, slice_ctx), 1)
+    even = (j == 2 * f).astype(jnp.float32).astype(jnp.bfloat16)
+    odd = (j == 2 * f + 1).astype(jnp.float32).astype(jnp.bfloat16)
+
+    def mix_block(b, carry):
+        zz, yy = b // 2, lax.rem(b, 2)
+        ctx = ctx_ref[zz, yy]
+        first = jnp.dot(ctx, even, preferred_element_type=jnp.float32)
+        second = jnp.dot(ctx, odd, preferred_element_type=jnp.float32)
+        scores = scores_ref[zz, yy]
+        routes = routes_ref[zz, yy]
+        g0 = jax.nn.sigmoid(scores[:, 0:1] - scores[:, 1:2])
+        first = first * g0
+        second = second * (1.0 - g0)
+        for x in range(experts):
+            value = jnp.where(routes[:, 0:1] == x, first, 0.0) + jnp.where(
+                routes[:, 1:2] == x, second, 0.0
+            )
+            mixed[zz, yy, :, x * slice_ctx : (x + 1) * slice_ctx] = value.astype(jnp.bfloat16)
+        return carry
+
+    lax.fori_loop(0, n_t, mix_block, 0)
+
+    def q_copy(c):
+        return send(q_send.at[c], q_recv.at[c], qs.at[c], qr.at[c], (e, other))
+
+    def s_copy(c, d):
+        to = lax.rem(z + d, n_z) * 2 + y
+        return send(s_send.at[c, d - 1], s_recv.at[c, d - 1], ss.at[c, d - 1], sr.at[c, d - 1], (e, to))
+
+    def pair_step(c, carry):
+        w_copy(c).wait()
+        block = mixed[:, 1 - y].reshape(n_z * rows, w.shape[1])
+        part = jnp.dot(block, w[c], preferred_element_type=jnp.float32)
+        q_send[c] = part.astype(jnp.bfloat16).reshape(n_z, rows, cols)
+        q_copy(c).start()
+        return carry
+
+    lax.fori_loop(0, n_c, pair_step, 0)
+
+    def own_step(c, carry):
+        block = mixed[:, y].reshape(n_z * rows, w.shape[1])
+        own[c] = jnp.dot(block, w[c], preferred_element_type=jnp.float32).reshape(n_z, rows, cols)
+        q_copy(c).wait_recv()
+        for d in range(1, n_z):
+            to = lax.rem(z + d, n_z)
+            s_send[c, d - 1] = (own[c, to] + q_recv[c, to].astype(jnp.float32)).astype(jnp.bfloat16)
+            s_copy(c, d).start()
+        return carry
+
+    lax.fori_loop(0, n_c, own_step, 0)
+
+    square = jnp.zeros((rows, 1), jnp.float32)
+    for c in range(n_c):
+        total = own[c, z] + q_recv[c, z].astype(jnp.float32)
+        for d in range(1, n_z):
+            s_copy(c, d).wait_recv()
+            total += s_recv[c, d - 1].astype(jnp.float32)
+        at = slice(c * cols, (c + 1) * cols)
+        piece = (resid_ref[:, at].astype(jnp.float32) + total).astype(jnp.bfloat16)
+        stream_ref[:, at] = piece
+        wide = piece.astype(jnp.float32)
+        square += jnp.sum(wide * wide, axis=1, keepdims=True)
+    width = resid_ref.shape[1]
+    scale = lax.rsqrt(square / width + norm_eps)
+    normed = (
+        stream_ref[...].astype(jnp.float32) * scale * gain_ref[...].astype(jnp.float32)
+    ).astype(jnp.bfloat16)
+    picked = jnp.dot(placer_ref[...], normed, preferred_element_type=jnp.float32)
+    d_send[...] = picked.astype(jnp.bfloat16).reshape(n_t, cap, width)
+
+    def d_copy(d):
+        to = lax.rem(t + d, n_t)
+        return send(d_send.at[to], held.at[e, t], ds.at[d], dr.at[d], (e, to))
+
+    for d in range(1, n_t):
+        d_copy(d).start()
+    held[e, t] = d_send[t]
+
+    def x_copy(d):
+        src = held.at[e, lax.rem(t + n_t - d, n_t)]
+        return send(src, src, xs.at[d], xr.at[d], (cross, t))
+
+    def c_copy(d):
+        src = held.at[e, lax.rem(t + n_t - d, n_t)]
+        return send(src, src, cs.at[d], cr.at[d], (sibling, t))
+
+    def f_copy(d):
+        src = held.at[cross, lax.rem(t + n_t - d, n_t)]
+        return send(src, src, fs.at[d], fr.at[d], (sibling, t))
+
+    for d in range(n_t):
+        if d:
+            d_copy(d).wait_recv()
+        x_copy(d).start()
+        c_copy(d).start()
+
+    logits = lax.dot_general(
+        normed, router_ref[...], (((1,), (1,)), ((), ())), preferred_element_type=jnp.float32
+    )
+    gap = jnp.sum(logits * pick_ref[...], axis=1, keepdims=True)
+    gate_ref[...] = jnp.broadcast_to(jax.nn.sigmoid(gap), gate_ref.shape)
+
+    for d in range(n_t):
+        x_copy(d).wait_recv()
+        f_copy(d).start()
+    for d in range(n_t):
+        c_copy(d).wait_recv()
+        f_copy(d).wait_recv()
+    out = pltpu.make_async_copy(held, rows_hbm, out_sem)
+    out.start()
+
+    def q_end(c, carry):
+        q_copy(c).wait_send()
+        for d in range(1, n_z):
+            s_copy(c, d).wait_send()
+        return carry
+
+    lax.fori_loop(0, n_c, q_end, 0)
+    for d in range(n_t):
+        if d:
+            d_copy(d).wait_send()
+        x_copy(d).wait_send()
+        c_copy(d).wait_send()
+        f_copy(d).wait_send()
+    out.wait()
+
+
+def back_kernel(
+    n_e, n_t, n_c, cap,
+    hidden_ref, w_hbm, stream_ref, gate_ref, take_ref, gain_ref,
+    out_ref, normal_ref,
+    w, a_send, a_recv, x_send, x_recv, own, r_send, back, after,
+    w_sem, as_, ar, xs, xr, rs, rr,
+):
+    e, t = lax.axis_index("expert"), lax.axis_index("tensor")
+    chip, core = e // 2, lax.rem(e, 2)
+    cross, sibling = lax.rem(e + 2, 4), e + 1 - 2 * core
+    rows = stream_ref.shape[0]
+    cols = w.shape[2]
+    group = n_t * cap
+
+    def w_copy(c):
+        return pltpu.make_async_copy(
+            w_hbm.at[:, pl.ds(c * cols, cols)], w.at[c], w_sem.at[c]
+        )
+
+    for c in range(n_c):
+        w_copy(c).start()
+    greet(n_e, n_t)
+
+    def a_copy(c):
+        return send(a_send.at[c], a_recv.at[c], as_.at[c], ar.at[c], (sibling, t))
+
+    def x_copy(c):
+        return send(x_send.at[c], x_recv.at[c], xs.at[c], xr.at[c], (cross, t))
+
+    def r_copy(c, d):
+        to = lax.rem(t + d, n_t)
+        return send(r_send.at[c, to], back.at[c, t], rs.at[c, d - 1], rr.at[c, d - 1], (e, to))
+
+    def sibling_step(c, carry):
+        w_copy(c).wait()
+        block = hidden_ref[:, 1 - core].reshape(2 * group, w.shape[1])
+        part = jnp.dot(block, w[c], preferred_element_type=jnp.float32)
+        a_send[c] = part.astype(jnp.bfloat16).reshape(2, group, cols)
+        a_copy(c).start()
+        return carry
+
+    lax.fori_loop(0, n_c, sibling_step, 0)
+
+    def own_step(c, carry):
+        block = hidden_ref[:, core].reshape(2 * group, w.shape[1])
+        own[c] = jnp.dot(block, w[c], preferred_element_type=jnp.float32).reshape(2, group, cols)
+        a_copy(c).wait_recv()
+        x_send[c] = (own[c, 1 - chip] + a_recv[c, 1 - chip].astype(jnp.float32)).astype(jnp.bfloat16)
+        x_copy(c).start()
+        return carry
+
+    lax.fori_loop(0, n_c, own_step, 0)
+
+    def return_step(c, carry):
+        x_copy(c).wait_recv()
+        total = own[c, chip] + a_recv[c, chip].astype(jnp.float32) + x_recv[c].astype(jnp.float32)
+        r_send[c] = total.astype(jnp.bfloat16).reshape(n_t, cap, cols)
+        for d in range(1, n_t):
+            r_copy(c, d).start()
+        back[c, t] = r_send[c, t]
+        return carry
+
+    lax.fori_loop(0, n_c, return_step, 0)
+
+    first = gate_ref[:, 0:1]
+    square = jnp.zeros((rows, 1), jnp.float32)
+    for c in range(n_c):
+        for d in range(1, n_t):
+            r_copy(c, d).wait_recv()
+        came = back[c].reshape(group, cols)
+        one = jnp.dot(take_ref[0], came, preferred_element_type=jnp.float32)
+        two = jnp.dot(take_ref[1], came, preferred_element_type=jnp.float32)
+        at = slice(c * cols, (c + 1) * cols)
+        value = stream_ref[:, at].astype(jnp.float32) + (one * first + two * (1.0 - first))
+        after[:, at] = value
+        out_ref[:, at] = value.astype(jnp.bfloat16)
+        square += jnp.sum(value * value, axis=1, keepdims=True)
+    scale = lax.rsqrt(square / stream_ref.shape[1] + norm_eps)
+    normal_ref[...] = (after[...] * scale * gain_ref[...].astype(jnp.float32)).astype(jnp.bfloat16)
+
+    def end(c, carry):
+        a_copy(c).wait_send()
+        x_copy(c).wait_send()
+        for d in range(1, n_t):
+            r_copy(c, d).wait_send()
+        return carry
+
+    lax.fori_loop(0, n_c, end, 0)
+
+
+def assign(mlp_routes, split_rule, placement, cap_blocks, expert_total, block_rows):
+    row_count, top_count = mlp_routes.shape
+    replicas = placement.shape[0]
+    slot_ids = jnp.arange(replicas, dtype=jnp.int32)
+    same = placement[None, :] == placement[:, None]
+    earlier = jnp.sum((same & (slot_ids[None, :] < slot_ids[:, None])).astype(jnp.int32), axis=1)
+    holds = placement[None, None, :] == mlp_routes[:, :, None]
+    route_copies = jnp.sum(holds.astype(jnp.int32), axis=2)
+    replica_rank = jnp.remainder(split_rule, route_copies)
+    match = (holds & (earlier[None, None, :] == replica_rank[:, :, None])).astype(jnp.int32)
+    slot = jnp.sum(match * slot_ids[None, None, :], axis=2)
+    capacity = jnp.sum(match * cap_blocks[None, None, :], axis=2) * block_rows
+    flat_match = match.reshape(row_count * top_count, replicas)
+    before = jnp.cumsum(flat_match, axis=0) - flat_match
+    arrival = jnp.sum(before * flat_match, axis=1).reshape(row_count, top_count)
+    return slot, arrival, arrival < capacity
+
+
+def fused_device(
+    resid, contexts, att_routes, att_scores, att_out_w, norm_gain, router_w, mlp_routes, split_rule,
+    placement, cap_blocks, w_gate_up, w_down, final_gain,
+):
+    n_t, n_e = lax.axis_size("tensor"), lax.axis_size("expert")
+    rows, width = resid.shape
+    n_z = n_t // 2
+    experts, slice_ctx = att_out_w.shape[0], att_out_w.shape[1]
+    top = att_routes.shape[1]
+    expert_total = router_w.shape[1]
+    block_rows = max(1, rows * top // (2 * placement.shape[0]))
+    cap = MAXB * block_rows
+    unit = w_down.shape[1]
+    slot, arrival, is_kept = assign(
+        mlp_routes, split_rule, placement, cap_blocks, expert_total, block_rows
+    )
+    position = jnp.where(is_kept, slot * cap + arrival, -1)
+    spots = jnp.arange(n_t * cap, dtype=jnp.int32)
+    take = (position.T[:, :, None] == spots[None, None, :]).astype(jnp.bfloat16)
+    placer = (
+        (spots[:, None] == position[None, :, 0]) | (spots[:, None] == position[None, :, 1])
+    ).astype(jnp.bfloat16)
+    expert_ids = jnp.arange(expert_total, dtype=jnp.int32)
+    pick = (mlp_routes[:, 0:1] == expert_ids[None, :]).astype(jnp.float32) - (
+        mlp_routes[:, 1:2] == expert_ids[None, :]
+    ).astype(jnp.float32)
+    bf16, f32, dma = jnp.bfloat16, jnp.float32, pltpu.SemaphoreType.DMA
+    vmem, anywhere = pl.BlockSpec(memory_space=pltpu.VMEM), pl.BlockSpec(memory_space=pl.ANY)
+
+    n_c = 8
+    cols = width // n_c
+    gathered, stream, gate = pl.pallas_call(
+        functools.partial(front_kernel, n_e, n_t, n_c, cap),
+        out_shape=(
+            jax.ShapeDtypeStruct((n_e, n_t, cap, width), bf16),
+            jax.ShapeDtypeStruct((rows, width), bf16),
+            jax.ShapeDtypeStruct((rows, 128), f32),
+        ),
+        in_specs=[vmem, vmem, vmem, anywhere] + [vmem] * 5,
+        out_specs=(anywhere, vmem, vmem),
+        scratch_shapes=[
+            pltpu.VMEM((n_c, experts * slice_ctx, cols), bf16),
+            pltpu.VMEM((n_z, 2, rows, experts * slice_ctx), bf16),
+            pltpu.VMEM((n_c, n_z, rows, cols), bf16),
+            pltpu.VMEM((n_c, n_z, rows, cols), bf16),
+            pltpu.VMEM((n_c, n_z - 1, rows, cols), bf16),
+            pltpu.VMEM((n_c, n_z - 1, rows, cols), bf16),
+            pltpu.VMEM((n_c, n_z, rows, cols), f32),
+            pltpu.VMEM((n_t, cap, width), bf16),
+            pltpu.VMEM((n_e, n_t, cap, width), bf16),
+            dma((n_c,)), dma, dma((n_c,)), dma((n_c,)),
+            dma((n_c, n_z - 1)), dma((n_c, n_z - 1)),
+        ] + [dma((n_t,))] * 8,
+        compiler_params=pltpu.CompilerParams(
+            collective_id=1, has_side_effects=True, vmem_limit_bytes=44 * 2**20
+        ),
+    )(
+        contexts.reshape(n_z, 2, rows, top * slice_ctx),
+        att_routes.reshape(n_z, 2, rows, top),
+        att_scores.reshape(n_z, 2, rows, top),
+        att_out_w.reshape(experts * slice_ctx, width),
+        resid,
+        norm_gain.reshape(1, width),
+        router_w.T,
+        pick,
+        placer,
+    )
+    hidden = activate(gathered[:, None], w_gate_up)
+    n_d = 4
+    wide = width // n_d
+    group = n_t * cap
+    return pl.pallas_call(
+        functools.partial(back_kernel, n_e, n_t, n_d, cap),
+        out_shape=(jax.ShapeDtypeStruct((rows, width), bf16),) * 2,
+        in_specs=[vmem, anywhere] + [vmem] * 4,
+        out_specs=(vmem, vmem),
+        scratch_shapes=[
+            pltpu.VMEM((n_d, unit, wide), bf16),
+            pltpu.VMEM((n_d, 2, group, wide), bf16),
+            pltpu.VMEM((n_d, 2, group, wide), bf16),
+            pltpu.VMEM((n_d, group, wide), bf16),
+            pltpu.VMEM((n_d, group, wide), bf16),
+            pltpu.VMEM((n_d, 2, group, wide), f32),
+            pltpu.VMEM((n_d, n_t, cap, wide), bf16),
+            pltpu.VMEM((n_d, n_t, cap, wide), bf16),
+            pltpu.VMEM((rows, width), f32),
+            dma((n_d,)), dma((n_d,)), dma((n_d,)), dma((n_d,)), dma((n_d,)),
+            dma((n_d, n_t - 1)), dma((n_d, n_t - 1)),
+        ],
+        compiler_params=pltpu.CompilerParams(
+            collective_id=2, has_side_effects=True, vmem_limit_bytes=44 * 2**20
+        ),
+    )(
+        hidden.reshape(n_e // 2, 2, group, unit),
+        w_down.reshape(unit, width),
+        stream,
+        gate,
+        take,
+        final_gain.reshape(1, width),
+    )
+
+
+def choose(*args):
+    n_t, n_e = lax.axis_size("tensor"), lax.axis_size("expert")
+    resid, placement = args[0], args[9]
+    replicas = placement.shape[0]
+    cap = MAXB * max(1, resid.shape[0] * args[2].shape[1] // (2 * replicas))
+    if n_e == 4 and n_t % 2 == 0 and n_t <= 8 and replicas == n_t and cap % 16 == 0:
+        return fused_device(*args)
+    return per_device(*args)
+
+
 def solution(mesh):
     return jax.shard_map(
-        per_device,
+        choose,
         mesh=mesh,
         in_specs=(
             P(("expert", "tensor"), None),

time: 212 us -> 111 us (0.52)
  waiting for transfers between devices: 135 us -> 0 us
  Pallas kernels: 0 us -> 83.6 us
  matrix products: 29.1 us -> 10.7 us
  blocking collectives: 16.8 us -> 0 us
  between operations: 14.1 us -> 0.81 us
  starting transfers between devices: 5.64 us -> 0 us
  local copies, waits for them, and re-layouts: 6.73 us -> 9.22 us
    reduce_scatter x2 -> x0, waiting for transfers between devices: 100 us -> none  [the longest x1 69.4 us: per_device(): lax.psum_scatter(jnp.dot(row_block, weight_flat, preferred_element_type=j...]
    pallas_call x0 -> x2, Pallas kernels: none -> 83.6 us  [the longest x1 56.3 us: fused_device(): pl.pallas_call(functools.partial(front_kernel, n_e, n_t, n_c, cap), out_s...]
    all_gather x1 -> x0, waiting for transfers between devices: 21.7 us -> none  [per_device(): arrived = lax.all_gather(landed[None], 'expert', axis=0, tiled=True)]
    dot_general x5 -> x0, matrix products: 17.7 us -> none  [the longest x1 7.47 us: per_device(): jnp.einsum('bsf,sfd->bsd', row_block, w_down, preferred_element_type=jnp....]
    all_to_all x1 -> x0, blocking collectives: 16.8 us -> none  [per_device(): lax.all_to_all(send_rows, 'tensor', split_axis=1, concat_axis=1, tiled=True)]
    all_to_all x1 -> x0, waiting for transfers between devices: 12.9 us -> none  [per_device(): lax.all_to_all(results, 'tensor', split_axis=0, concat_axis=0, tiled=True)]
    all_to_all x1 -> x0, starting transfers between devices: 5.52 us -> none  [per_device(): lax.all_to_all(results, 'tensor', split_axis=0, concat_axis=0, tiled=True)]
    unnamed x25 -> x17, local copies, waits for them, and re-layouts: 1.56 us -> 6.6 us
  transfers between devices with their start and end apart: 4 -> 0, of which waited for: 4 -> 0; matrix products, arithmetic and copies ran while one was open for 2% -> 0% of each run, Pallas kernels for 0% -> 0%
where the time goes in v2:
time: 111 us; the launch traced here: 110 us
  Pallas kernels  83.6 us (75%)
  matrix products  10.7 us (10%)
  local copies, waits for them, and re-layouts  9.22 us (8%)
  other arithmetic  6.02 us (5%)
    pallas_call x1, Pallas kernels, fused_device(): pl.pallas_call(functools.partial(front_kernel, n_e, n_t, n_c, cap), out_s...  56.3 us
    pallas_call x1, Pallas kernels, fused_device(): pl.pallas_call(functools.partial(back_kernel, n_e, n_t, n_d, cap), out_sh...  27.4 us
    dot_general x1, matrix products, activate(): jnp.einsum('tsecd,sdgf->tsecgf', shard_piece, w_gate_up, preferred_elemen...  10.7 us
    unnamed x17, local copies, waits for them, and re-layouts  6.6 us

profile of v2, /device:TPU:0, one launch (start us, length us, event | category | flops | bytes accessed | tf_op | source)
XLA Modules:
  0.0 110.4 jit_solution(17283327960401340945)
XLA Ops:
  0.6 0.8 fusion.10
  1.4 0.8 and_select_fusion
  2.3 0.1 eq.155
  2.4 0.9 convert_reduce_fusion
  3.4 0.8 copy.42
  4.3 0.8 fusion.9
  5.0 0.2 reduce_window_sum.11
  5.2 0.8 select_reduce_fusion
  6.0 0.1 reshape.70
  6.3 0.8 select_reduce_fusion.2
  7.1 0.8 slice_bitcast_fusion.2
  7.9 0.8 copy.39
  8.8 0.8 copy.40
  9.6 0.7 reshape.69.gain_ref
  10.3 1.0 copy-done
  11.4 0.9 copy-done.1
  12.3 0.8 copy-done.2
  13.1 56.3 %shard_map.149 = (bf16[4,8,16,2048]{3,2,1,0:T(8,128)(2,1)S(1)}, bf16[64,2048]{1,0:T(8,128)(2,1)S(1)}, f32[64,128]{1,0:T(8,128)S(1)}) custom-call(bf16[4,2,64,512]{3,2,1,0:T(8,128)(2,1)S(1)} %bitcast.36, s32[4,2,64,2]{3,2,1,0:T(8,128)S(1)} %bitcast.34, f32[4,2,64,2]{3,2,1,0:T(8,128)S(1)} %bitcast.35, bf16[2048,2048]{1,0:T(8,128)(2,1)} %bitcast.40, ...), custom_call_target="tpu_custom_call" | custom-call | tf_op jit(solution)/shard_map/pallas_call | solution.py:474
  69.4 10.7 %fusion.2 = f32[4,1,8,16,2,1408]{5,3,4,2,0,1:T(8,128)S(1)} fusion(bf16[2048,2,1408,1,1]{2,1,0,4,3:T(2,128)(2,1)} %bitcast.42, bf16[4,8,16,2048]{3,2,1,0:T(8,128)(2,1)S(1)} %get-tuple-element.5), kind=kOutput, calls=%fused_computation.2 | convolution fusion | flops 5905580032 | bytes 19398656 | tf_op jit(solution)/shard_map/tsecd,sdgf->tsecgf/dot_general | solution.py:32
  80.1 0.6 fusion.12
  80.7 0.8 multiply_convert_fusion.hidden_ref
  81.6 27.4 %shard_map.150 = (bf16[64,2048]{1,0:T(8,128)(2,1)S(1)}, bf16[64,2048]{1,0:T(8,128)(2,1)S(1)}) custom-call(bf16[2,2,128,1408]{3,2,1,0:T(8,128)(2,1)S(1)} %multiply_convert_fusion.hidden_ref, bf16[1408,2048]{1,0:T(8,128)(2,1)S(1)} %bitcast.33, bf16[64,2048]{1,0:T(8,128)(2,1)S(1)} %get-tuple-element.6.stream_ref, f32[64,128]{1,0:T(8,128)S(1)} %get-tuple-element.7.gate_ref, ...), custom_call_target="tpu_custom_call" | custom-call | tf_op jit(solution)/shard_map/pallas_call | solution.py:514
  109.0 0.7 copy.57
  109.7 0.7 copy.58
  (19 shorter events, 0.5 us)
Async XLA Ops:
  10.3 1.0 copy-start
  11.4 0.9 copy-start.1
  12.3 0.8 copy-start.2
  69.3 12.2 %slice-start = ((s8[5767168]{0:T(1024)(128)(4,1)}), s8[4194304]{0:T(1024)(128)(4,1)S(1)}, s32[]{:S(2)}) async-start(s8[5767168]{0:T(1024)(128)(4,1)} %bitcast.31), calls=%async_computation | async-start | bytes 8388608
  69.4 12.2 %slice-start.1 = ((s8[5767168]{0:T(1024)(128)(4,1)}), s8[1572864]{0:T(1024)(128)(4,1)S(1)}, s32[]{:S(2)}) async-start(s8[5767168]{0:T(1024)(128)(4,1)} %bitcast.31), calls=%async_computation.1 | async-start | bytes 3145728
  80.7 0.9 copy-start.3

commit v3 on v2

--- a/solution.py
+++ b/solution.py
@@ -177,10 +177,57 @@
     )
 
 
+def column(row):
+    n = row.shape[1]
+    i = lax.broadcasted_iota(jnp.int32, (n, n), 0)
+    j = lax.broadcasted_iota(jnp.int32, (n, n), 1)
+    return jnp.sum(jnp.where(i == j, row, 0.0), axis=1, keepdims=True)
+
+
+def assign(routes, splits, place_ref, blocks_ref, block_rows, cap):
+    replicas = place_ref.shape[0]
+    place = [place_ref[r] for r in range(replicas)]
+    limit = [(blocks_ref[r] * block_rows).astype(jnp.float32) for r in range(replicas)]
+    earlier = [
+        sum(((place[q] == place[r]).astype(jnp.int32) for q in range(r)), jnp.int32(0)).astype(
+            jnp.float32
+        )
+        for r in range(replicas)
+    ]
+    place = [p.astype(jnp.float32) for p in place]
+    rows = routes[0].shape[0]
+    lane = lax.broadcasted_iota(jnp.int32, (rows, replicas), 1)
+    matches, slots, limits = [], [], []
+    for route, split in zip(routes, splits):
+        held_by = [(route == p).astype(jnp.float32) for p in place]
+        copies = sum(held_by)
+        rank = split - copies * jnp.floor((split + 0.5) / copies)
+        hits = [h * (rank == q).astype(jnp.float32) for h, q in zip(held_by, earlier)]
+        match = jnp.zeros((rows, replicas), jnp.float32)
+        for r, hit in enumerate(hits):
+            match += jnp.where(lane == r, hit, 0.0)
+        matches.append(match)
+        slots.append(sum(hit * float(r) for r, hit in enumerate(hits)))
+        limits.append(sum(hit * m for hit, m in zip(hits, limit)))
+    i = lax.broadcasted_iota(jnp.int32, (rows, rows), 0)
+    j = lax.broadcasted_iota(jnp.int32, (rows, rows), 1)
+    lower = (j < i).astype(jnp.float32)
+    before = jnp.dot(lower, matches[0] + matches[1], preferred_element_type=jnp.float32)
+    befores = (before, before + matches[0])
+    spot = lax.broadcasted_iota(jnp.int32, (rows, replicas * cap), 1).astype(jnp.float32)
+    taken = []
+    for k in range(2):
+        arrival = jnp.sum(befores[k] * matches[k], axis=1, keepdims=True)
+        position = jnp.where(arrival < limits[k], slots[k] * cap + arrival, -1.0)
+        taken.append((spot == position).astype(jnp.float32))
+    return taken
+
+
 def front_kernel(
     n_e, n_t, n_c, cap,
-    ctx_ref, routes_ref, scores_ref, w_hbm, resid_ref, gain_ref, router_ref, pick_ref, placer_ref,
-    rows_hbm, stream_ref, gate_ref,
+    ctx_ref, routes_ref, scores_ref, w_hbm, resid_ref, gain_ref, router_ref,
+    chosen_ref, split_ref, place_ref, blocks_ref,
+    rows_hbm, stream_ref, gate_ref, take_ref,
     w, mixed, q_send, q_recv, s_send, s_recv, own, d_send, held,
     w_sem, out_sem, qs, qr, ss, sr, ds, dr, xs, xr, cs, cr, fs, fr,
 ):
@@ -208,24 +255,25 @@
     even = (j == 2 * f).astype(jnp.float32).astype(jnp.bfloat16)
     odd = (j == 2 * f + 1).astype(jnp.float32).astype(jnp.bfloat16)
 
-    def mix_block(b, carry):
-        zz, yy = b // 2, lax.rem(b, 2)
-        ctx = ctx_ref[zz, yy]
+    def mix_block(zz, carry):
+        ctx = ctx_ref[zz].reshape(2 * rows, 2 * slice_ctx)
         first = jnp.dot(ctx, even, preferred_element_type=jnp.float32)
         second = jnp.dot(ctx, odd, preferred_element_type=jnp.float32)
-        scores = scores_ref[zz, yy]
-        routes = routes_ref[zz, yy]
-        g0 = jax.nn.sigmoid(scores[:, 0:1] - scores[:, 1:2])
+        at = pl.ds(pl.multiple_of(zz * 2 * rows, 2 * rows), 2 * rows)
+        scores = scores_ref[:, at]
+        routes = routes_ref[:, at].astype(jnp.float32)
+        g0 = column(jax.nn.sigmoid(scores[0:1] - scores[1:2]))
+        r0, r1 = column(routes[0:1]), column(routes[1:2])
         first = first * g0
         second = second * (1.0 - g0)
         for x in range(experts):
-            value = jnp.where(routes[:, 0:1] == x, first, 0.0) + jnp.where(
-                routes[:, 1:2] == x, second, 0.0
-            )
-            mixed[zz, yy, :, x * slice_ctx : (x + 1) * slice_ctx] = value.astype(jnp.bfloat16)
-        return carry
-
-    lax.fori_loop(0, n_t, mix_block, 0)
+            value = jnp.where(r0 == x, first, 0.0) + jnp.where(r1 == x, second, 0.0)
+            mixed[zz, :, :, x * slice_ctx : (x + 1) * slice_ctx] = value.astype(
+                jnp.bfloat16
+            ).reshape(2, rows, slice_ctx)
+        return carry
+
+    lax.fori_loop(0, n_z, mix_block, 0)
 
     def q_copy(c):
         return send(q_send.at[c], q_recv.at[c], qs.at[c], qr.at[c], (e, other))
@@ -243,6 +291,12 @@
         return carry
 
     lax.fori_loop(0, n_c, pair_step, 0)
+
+    routes = [column(chosen_ref[k : k + 1].astype(jnp.float32)) for k in range(2)]
+    splits = [column(split_ref[k : k + 1].astype(jnp.float32)) for k in range(2)]
+    taken = assign(routes, splits, place_ref, blocks_ref, cap // MAXB, cap)
+    for k in range(2):
+        take_ref[k] = taken[k].astype(jnp.bfloat16)
 
     def own_step(c, carry):
         block = mixed[:, y].reshape(n_z * rows, w.shape[1])
@@ -272,7 +326,12 @@
     normed = (
         stream_ref[...].astype(jnp.float32) * scale * gain_ref[...].astype(jnp.float32)
     ).astype(jnp.bfloat16)
-    picked = jnp.dot(placer_ref[...], normed, preferred_element_type=jnp.float32)
+    picked = lax.dot_general(
+        (taken[0] + taken[1]).astype(jnp.bfloat16),
+        normed,
+        (((0,), (0,)), ((), ())),
+        preferred_element_type=jnp.float32,
+    )
     d_send[...] = picked.astype(jnp.bfloat16).reshape(n_t, cap, width)
 
     def d_copy(d):
@@ -304,7 +363,9 @@
     logits = lax.dot_general(
         normed, router_ref[...], (((1,), (1,)), ((), ())), preferred_element_type=jnp.float32
     )
-    gap = jnp.sum(logits * pick_ref[...], axis=1, keepdims=True)
+    expert = lax.broadcasted_iota(jnp.int32, logits.shape, 1).astype(jnp.float32)
+    pick = (expert == routes[0]).astype(jnp.float32) - (expert == routes[1]).astype(jnp.float32)
+    gap = jnp.sum(logits * pick, axis=1, keepdims=True)
     gate_ref[...] = jnp.broadcast_to(jax.nn.sigmoid(gap), gate_ref.shape)
 
     for d in range(n_t):
@@ -422,24 +483,6 @@
     lax.fori_loop(0, n_c, end, 0)
 
 
-def assign(mlp_routes, split_rule, placement, cap_blocks, expert_total, block_rows):
-    row_count, top_count = mlp_routes.shape
-    replicas = placement.shape[0]
-    slot_ids = jnp.arange(replicas, dtype=jnp.int32)
-    same = placement[None, :] == placement[:, None]
-    earlier = jnp.sum((same & (slot_ids[None, :] < slot_ids[:, None])).astype(jnp.int32), axis=1)
-    holds = placement[None, None, :] == mlp_routes[:, :, None]
-    route_copies = jnp.sum(holds.astype(jnp.int32), axis=2)
-    replica_rank = jnp.remainder(split_rule, route_copies)
-    match = (holds & (earlier[None, None, :] == replica_rank[:, :, None])).astype(jnp.int32)
-    slot = jnp.sum(match * slot_ids[None, None, :], axis=2)
-    capacity = jnp.sum(match * cap_blocks[None, None, :], axis=2) * block_rows
-    flat_match = match.reshape(row_count * top_count, replicas)
-    before = jnp.cumsum(flat_match, axis=0) - flat_match
-    arrival = jnp.sum(before * flat_match, axis=1).reshape(row_count, top_count)
-    return slot, arrival, arrival < capacity
-
-
 def fused_device(
     resid, contexts, att_routes, att_scores, att_out_w, norm_gain, router_w, mlp_routes, split_rule,
     placement, cap_blocks, w_gate_up, w_down, final_gain,
@@ -449,37 +492,24 @@
     n_z = n_t // 2
     experts, slice_ctx = att_out_w.shape[0], att_out_w.shape[1]
     top = att_routes.shape[1]
-    expert_total = router_w.shape[1]
-    block_rows = max(1, rows * top // (2 * placement.shape[0]))
-    cap = MAXB * block_rows
+    cap = MAXB * max(1, rows * top // (2 * placement.shape[0]))
     unit = w_down.shape[1]
-    slot, arrival, is_kept = assign(
-        mlp_routes, split_rule, placement, cap_blocks, expert_total, block_rows
-    )
-    position = jnp.where(is_kept, slot * cap + arrival, -1)
-    spots = jnp.arange(n_t * cap, dtype=jnp.int32)
-    take = (position.T[:, :, None] == spots[None, None, :]).astype(jnp.bfloat16)
-    placer = (
-        (spots[:, None] == position[None, :, 0]) | (spots[:, None] == position[None, :, 1])
-    ).astype(jnp.bfloat16)
-    expert_ids = jnp.arange(expert_total, dtype=jnp.int32)
-    pick = (mlp_routes[:, 0:1] == expert_ids[None, :]).astype(jnp.float32) - (
-        mlp_routes[:, 1:2] == expert_ids[None, :]
-    ).astype(jnp.float32)
     bf16, f32, dma = jnp.bfloat16, jnp.float32, pltpu.SemaphoreType.DMA
+    smem = pl.BlockSpec(memory_space=pltpu.SMEM)
     vmem, anywhere = pl.BlockSpec(memory_space=pltpu.VMEM), pl.BlockSpec(memory_space=pl.ANY)
 
     n_c = 8
     cols = width // n_c
-    gathered, stream, gate = pl.pallas_call(
+    gathered, stream, gate, take = pl.pallas_call(
         functools.partial(front_kernel, n_e, n_t, n_c, cap),
         out_shape=(
             jax.ShapeDtypeStruct((n_e, n_t, cap, width), bf16),
             jax.ShapeDtypeStruct((rows, width), bf16),
             jax.ShapeDtypeStruct((rows, 128), f32),
+            jax.ShapeDtypeStruct((top, rows, n_t * cap), bf16),
         ),
-        in_specs=[vmem, vmem, vmem, anywhere] + [vmem] * 5,
-        out_specs=(anywhere, vmem, vmem),
+        in_specs=[vmem, vmem, vmem, anywhere] + [vmem] * 5 + [smem] * 2,
+        out_specs=(anywhere, vmem, vmem, vmem),
         scratch_shapes=[
             pltpu.VMEM((n_c, experts * slice_ctx, cols), bf16),
             pltpu.VMEM((n_z, 2, rows, experts * slice_ctx), bf16),
@@ -498,14 +528,16 @@
         ),
     )(
         contexts.reshape(n_z, 2, rows, top * slice_ctx),
-        att_routes.reshape(n_z, 2, rows, top),
-        att_scores.reshape(n_z, 2, rows, top),
+        att_routes.T,
+        att_scores.T,
         att_out_w.reshape(experts * slice_ctx, width),
         resid,
         norm_gain.reshape(1, width),
         router_w.T,
-        pick,
-        placer,
+        mlp_routes.T,
+        split_rule.T,
+        placement,
+        cap_blocks,
     )
     hidden = activate(gathered[:, None], w_gate_up)
     n_d = 4
@@ -545,9 +577,9 @@
 def choose(*args):
     n_t, n_e = lax.axis_size("tensor"), lax.axis_size("expert")
     resid, placement = args[0], args[9]
-    replicas = placement.shape[0]
+    replicas, rows = placement.shape[0], resid.shape[0]
     cap = MAXB * max(1, resid.shape[0] * args[2].shape[1] // (2 * replicas))
-    if n_e == 4 and n_t % 2 == 0 and n_t <= 8 and replicas == n_t and cap % 16 == 0:
+    if n_e == 4 and n_t % 2 == 0 and n_t <= 8 and replicas == n_t and cap % 16 == 0 and rows % 64 == 0:
         return fused_device(*args)
     return per_device(*args)
 

time: 111 us -> 106 us (0.955)
  other arithmetic: 6.02 us -> 0.79 us
    reduce_sum x4 -> x0, other arithmetic: 3.31 us -> none  [the longest x1 0.92 us: assign(): jnp.sum((same & (slot_ids[None, :] < slot_ids[:, None])).astype(jnp.int32...]
    unnamed x17 -> x26, local copies, waits for them, and re-layouts: 6.6 us -> 8.21 us
where the time goes in v3:
time: 106 us; the launch traced here: 105 us
  Pallas kernels  83.5 us (79%)
  matrix products  10.7 us (10%)
  local copies, waits for them, and re-layouts  9.46 us (9%)
    pallas_call x1, Pallas kernels, fused_device(): pl.pallas_call(functools.partial(front_kernel, n_e, n_t, n_c, cap), out_s...  56 us
    pallas_call x1, Pallas kernels, fused_device(): pl.pallas_call(functools.partial(back_kernel, n_e, n_t, n_d, cap), out_sh...  27.4 us
    dot_general x1, matrix products, activate(): jnp.einsum('tsecd,sdgf->tsecgf', shard_piece, w_gate_up, preferred_elemen...  10.7 us
    unnamed x26, local copies, waits for them, and re-layouts  8.21 us

profile of v3, /device:TPU:0, one launch (start us, length us, event | category | flops | bytes accessed | tf_op | source)
XLA Modules:
  0.0 105.1 jit_solution(17694940135750516599)
XLA Ops:
  0.6 0.7 reshape.43.gain_ref
  1.3 0.0 copy-start
  1.3 1.0 copy-done
  2.4 0.0 copy-start.1
  2.4 0.9 copy-done.1
  3.3 0.8 copy-done.2
  4.1 0.7 copy-done.3
  4.8 0.7 copy-done.4
  5.5 0.7 copy-done.5
  6.1 0.7 copy-done.6
  6.8 0.7 copy-done.7
  7.5 0.7 copy-done.8
  8.1 56.0 %shard_map.149 = (bf16[4,8,16,2048]{3,2,1,0:T(8,128)(2,1)S(1)}, bf16[64,2048]{1,0:T(8,128)(2,1)S(1)}, f32[64,128]{1,0:T(8,128)S(1)}, bf16[2,64,128]{2,1,0:T(8,128)(2,1)S(1)}) custom-call(bf16[4,2,64,512]{3,2,1,0:T(8,128)(2,1)S(1)} %bitcast.27, s32[2,512]{1,0:T(2,128)S(1)} %bitcast.29, f32[2,512]{1,0:T(2,128)S(1)} %bitcast.30, bf16[2048,2048]{1,0:T(8,128)(2,1)} %bitcast.35, ...), custom_call_target="tpu_custom_call" | custom-call | tf_op jit(solution)/shard_map/pallas_call | solution.py:503
  64.2 0.0 slice-start.1
  64.2 10.7 %fusion.2 = f32[4,1,8,16,2,1408]{5,3,4,2,0,1:T(8,128)S(1)} fusion(bf16[2048,2,1408,1,1]{2,1,0,4,3:T(2,128)(2,1)} %bitcast.36, bf16[4,8,16,2048]{3,2,1,0:T(8,128)(2,1)S(1)} %get-tuple-element.6), kind=kOutput, calls=%fused_computation.2 | convolution fusion | flops 5905580032 | bytes 19398656 | tf_op jit(solution)/shard_map/tsecd,sdgf->tsecgf/dot_general | solution.py:32
  74.8 0.6 fusion.6
  75.4 0.0 copy-start.9
  75.4 0.8 multiply_convert_fusion.hidden_ref
  76.2 0.0 copy-done.9
  76.2 0.0 slice-done
  76.2 0.0 slice-done.1
  76.3 27.4 %shard_map.150 = (bf16[64,2048]{1,0:T(8,128)(2,1)S(1)}, bf16[64,2048]{1,0:T(8,128)(2,1)S(1)}) custom-call(bf16[2,2,128,1408]{3,2,1,0:T(8,128)(2,1)S(1)} %multiply_convert_fusion.hidden_ref, bf16[1408,2048]{1,0:T(8,128)(2,1)S(1)} %bitcast.26, bf16[64,2048]{1,0:T(8,128)(2,1)S(1)} %get-tuple-element.7.stream_ref, f32[64,128]{1,0:T(8,128)S(1)} %get-tuple-element.8.gate_ref, ...), custom_call_target="tpu_custom_call" | custom-call | tf_op jit(solution)/shard_map/pallas_call | solution.py:546
  103.7 0.7 copy.27
  104.4 0.7 copy.28
  (10 shorter events, 0.0 us)
Async XLA Ops:
  1.3 1.0 copy-start
  2.4 0.9 copy-start.1
  3.3 0.8 copy-start.2
  4.1 0.7 copy-start.3
  4.8 0.7 copy-start.4
  5.4 0.7 copy-start.5
  6.1 0.7 copy-start.6
  6.8 0.7 copy-start.7
  7.5 0.7 copy-start.8
  8.1 68.1 %slice-start = ((s8[5767168]{0:T(1024)(128)(4,1)}), s8[1572864]{0:T(1024)(128)(4,1)S(1)}, s32[]{:S(2)}) async-start(s8[5767168]{0:T(1024)(128)(4,1)} %bitcast.24), calls=%async_computation | async-start | bytes 3145728
  64.2 12.1 %slice-start.1 = ((s8[5767168]{0:T(1024)(128)(4,1)}), s8[4194304]{0:T(1024)(128)(4,1)S(1)}, s32[]{:S(2)}) async-start(s8[5767168]{0:T(1024)(128)(4,1)} %bitcast.24), calls=%async_computation.1 | async-start | bytes 8388608
  75.4 0.8 copy-start.9

commit v4 on v3

--- a/solution.py
+++ b/solution.py
@@ -163,7 +163,7 @@
         pl.semaphore_signal(
             barrier, inc=1, device_id=(lax.rem(e + d, n_e), t), device_id_type=MESH
         )
-    pl.semaphore_wait(barrier, n_t + n_e - 2)
+    return barrier, n_t + n_e - 2
 
 
 def send(src, dst, send_sem, recv_sem, device):
@@ -225,9 +225,11 @@
 
 def front_kernel(
     n_e, n_t, n_c, cap,
-    ctx_ref, routes_ref, scores_ref, w_hbm, resid_ref, gain_ref, router_ref,
-    chosen_ref, split_ref, place_ref, blocks_ref,
+    ctx_hbm, routes_hbm, scores_hbm, w_hbm, resid_hbm, gain_hbm, router_hbm,
+    chosen_hbm, split_hbm, place_hbm, blocks_hbm,
     rows_hbm, stream_ref, gate_ref, take_ref,
+    ctx_ref, routes_ref, scores_ref, resid_ref, gain_ref, router_ref,
+    chosen_ref, split_ref, place_ref, blocks_ref, in_sem,
     w, mixed, q_send, q_recv, s_send, s_recv, own, d_send, held,
     w_sem, out_sem, qs, qr, ss, sr, ds, dr, xs, xr, cs, cr, fs, fr,
 ):
@@ -246,9 +248,30 @@
             w_hbm.at[:, pl.ds(c * cols, cols)], w.at[c], w_sem.at[c]
         )
 
+    loads = [
+        pltpu.make_async_copy(far, near, in_sem.at[i])
+        for i, (far, near) in enumerate(
+            (
+                (ctx_hbm, ctx_ref),
+                (routes_hbm, routes_ref),
+                (scores_hbm, scores_ref),
+                (resid_hbm, resid_ref),
+                (gain_hbm, gain_ref),
+                (router_hbm, router_ref),
+                (chosen_hbm, chosen_ref),
+                (split_hbm, split_ref),
+                (place_hbm, place_ref),
+                (blocks_hbm, blocks_ref),
+            )
+        )
+    ]
+    for load in loads:
+        load.start()
     for c in range(n_c):
         w_copy(c).start()
-    greet(n_e, n_t)
+    barrier, guests = greet(n_e, n_t)
+    for load in loads:
+        load.wait()
 
     j = lax.broadcasted_iota(jnp.int32, (2 * slice_ctx, slice_ctx), 0)
     f = lax.broadcasted_iota(jnp.int32, (2 * slice_ctx, slice_ctx), 1)
@@ -274,6 +297,7 @@
         return carry
 
     lax.fori_loop(0, n_z, mix_block, 0)
+    pl.semaphore_wait(barrier, guests)
 
     def q_copy(c):
         return send(q_send.at[c], q_recv.at[c], qs.at[c], qr.at[c], (e, other))
@@ -414,7 +438,7 @@
 
     for c in range(n_c):
         w_copy(c).start()
-    greet(n_e, n_t)
+    pl.semaphore_wait(*greet(n_e, n_t))
 
     def a_copy(c):
         return send(a_send.at[c], a_recv.at[c], as_.at[c], ar.at[c], (sibling, t))
@@ -492,10 +516,10 @@
     n_z = n_t // 2
     experts, slice_ctx = att_out_w.shape[0], att_out_w.shape[1]
     top = att_routes.shape[1]
+    expert_total = router_w.shape[1]
     cap = MAXB * max(1, rows * top // (2 * placement.shape[0]))
     unit = w_down.shape[1]
     bf16, f32, dma = jnp.bfloat16, jnp.float32, pltpu.SemaphoreType.DMA
-    smem = pl.BlockSpec(memory_space=pltpu.SMEM)
     vmem, anywhere = pl.BlockSpec(memory_space=pltpu.VMEM), pl.BlockSpec(memory_space=pl.ANY)
 
     n_c = 8
@@ -508,9 +532,20 @@
             jax.ShapeDtypeStruct((rows, 128), f32),
             jax.ShapeDtypeStruct((top, rows, n_t * cap), bf16),
         ),
-        in_specs=[vmem, vmem, vmem, anywhere] + [vmem] * 5 + [smem] * 2,
+        in_specs=[anywhere] * 11,
         out_specs=(anywhere, vmem, vmem, vmem),
         scratch_shapes=[
+            pltpu.VMEM((n_z, 2, rows, top * slice_ctx), bf16),
+            pltpu.VMEM((top, n_t * rows), jnp.int32),
+            pltpu.VMEM((top, n_t * rows), f32),
+            pltpu.VMEM((rows, width), bf16),
+            pltpu.VMEM((1, width), bf16),
+            pltpu.VMEM((expert_total, width), bf16),
+            pltpu.VMEM((top, rows), jnp.int32),
+            pltpu.VMEM((top, rows), jnp.int32),
+            pltpu.SMEM(placement.shape, jnp.int32),
+            pltpu.SMEM(cap_blocks.shape, jnp.int32),
+            dma((10,)),
             pltpu.VMEM((n_c, experts * slice_ctx, cols), bf16),
             pltpu.VMEM((n_z, 2, rows, experts * slice_ctx), bf16),
             pltpu.VMEM((n_c, n_z, rows, cols), bf16),
@@ -524,7 +559,7 @@
             dma((n_c, n_z - 1)), dma((n_c, n_z - 1)),
         ] + [dma((n_t,))] * 8,
         compiler_params=pltpu.CompilerParams(
-            collective_id=1, has_side_effects=True, vmem_limit_bytes=44 * 2**20
+            collective_id=1, has_side_effects=True, vmem_limit_bytes=60 * 2**20
         ),
     )(
         contexts.reshape(n_z, 2, rows, top * slice_ctx),

time: 106 us -> 100 us (0.943)
  local copies, waits for them, and re-layouts: 9.46 us -> 3.3 us
    unnamed x26 -> x14, local copies, waits for them, and re-layouts: 8.21 us -> 1.53 us
where the time goes in v4:
time: 100 us; the launch traced here: 99.9 us
  Pallas kernels  83.7 us (84%)
  matrix products  11.3 us (11%)
  local copies, waits for them, and re-layouts  3.3 us (3%)
    pallas_call x1, Pallas kernels, fused_device(): pl.pallas_call(functools.partial(front_kernel, n_e, n_t, n_c, cap), out_s...  56.9 us
    pallas_call x1, Pallas kernels, fused_device(): pl.pallas_call(functools.partial(back_kernel, n_e, n_t, n_d, cap), out_sh...  26.8 us
    dot_general x1, matrix products, activate(): jnp.einsum('tsecd,sdgf->tsecgf', shard_piece, w_gate_up, preferred_elemen...  11.3 us

profile of v4, /device:TPU:0, one launch (start us, length us, event | category | flops | bytes accessed | tf_op | source)
XLA Modules:
  0.0 99.9 jit_solution(5451341012641174397)
XLA Ops:
  0.6 1.3 %reshape.43.gain_hbm = bf16[1,2048]{1,0:T(2,128)(2,1)} reshape(bf16[2048]{0:T(1024)(128)(2,1)} %param.19) | data formatting | bytes 8192 | tf_op jit(solution)/shard_map/reshape | solution.py:570
  1.9 0.0 slice-start
  1.9 56.9 %shard_map.149 = (bf16[4,8,16,2048]{3,2,1,0:T(8,128)(2,1)}, bf16[64,2048]{1,0:T(8,128)(2,1)}, f32[64,128]{1,0:T(8,128)}, bf16[2,64,128]{2,1,0:T(8,128)(2,1)}) custom-call(bf16[4,2,64,512]{3,2,1,0:T(8,128)(2,1)} %bitcast.30, s32[2,512]{1,0:T(2,128)} %bitcast.32, f32[2,512]{1,0:T(2,128)} %bitcast.33, bf16[2048,2048]{1,0:T(8,128)(2,1)} %bitcast.29, ...), custom_call_target="tpu_custom_call" | custom-call | tf_op jit(solution)/shard_map/pallas_call | solution.py:527
  58.8 0.0 slice-start.1
  58.9 11.3 %fusion.2 = f32[4,1,8,16,2,1408]{5,3,4,2,0,1:T(8,128)S(1)} fusion(bf16[2048,2,1408,1,1]{2,1,0,4,3:T(2,128)(2,1)} %bitcast.36, bf16[4,8,16,2048]{3,2,1,0:T(8,128)(2,1)} %get-tuple-element.6), kind=kOutput, calls=%fused_computation.2 | convolution fusion | flops 5905580032 | bytes 19398656 | tf_op jit(solution)/shard_map/tsecd,sdgf->tsecgf/dot_general | solution.py:32
  70.2 0.5 fusion.6
  70.7 0.0 copy-start.3
  70.7 0.0 copy-start
  70.7 0.0 copy-start.1
  70.7 0.0 copy-start.2
  70.7 0.8 multiply_convert_fusion.hidden_ref
  71.5 0.0 copy-done.3
  71.6 0.0 slice-done
  71.6 0.0 slice-done.1
  71.6 0.1 copy-done
  71.7 0.0 copy-done.1
  71.7 0.0 copy-done.2
  71.7 26.8 %shard_map.150 = (bf16[64,2048]{1,0:T(8,128)(2,1)S(1)}, bf16[64,2048]{1,0:T(8,128)(2,1)S(1)}) custom-call(bf16[2,2,128,1408]{3,2,1,0:T(8,128)(2,1)S(1)} %multiply_convert_fusion.hidden_ref, bf16[1408,2048]{1,0:T(8,128)(2,1)S(1)} %bitcast.26, bf16[64,2048]{1,0:T(8,128)(2,1)S(1)} %copy-done, f32[64,128]{1,0:T(8,128)S(1)} %copy-done.1, ...), custom_call_target="tpu_custom_call" | custom-call | tf_op jit(solution)/shard_map/pallas_call | solution.py:581
  98.5 0.7 copy.27
  99.2 0.7 copy.28
  (2 shorter events, 0.0 us)
Async XLA Ops:
  1.9 69.6 %slice-start = ((s8[5767168]{0:T(1024)(128)(4,1)}), s8[1572864]{0:T(1024)(128)(4,1)S(1)}, s32[]{:S(2)}) async-start(s8[5767168]{0:T(1024)(128)(4,1)} %bitcast.24), calls=%async_computation | async-start | bytes 3145728
  58.8 12.7 %slice-start.1 = ((s8[5767168]{0:T(1024)(128)(4,1)}), s8[4194304]{0:T(1024)(128)(4,1)S(1)}, s32[]{:S(2)}) async-start(s8[5767168]{0:T(1024)(128)(4,1)} %bitcast.24), calls=%async_computation.1 | async-start | bytes 8388608
  70.7 0.8 copy-start.3
  70.7 1.0 copy-start
  70.7 0.9 copy-start.1
  70.7 0.9 copy-start.2
